TPU v7x, 32 devices: a whole 2x2x4 slice. The times are simulated.
32 devices in a mesh: ctx: 8 (over z, x), tp: 4 (over y, core).
Axes of the slice: x: 2, y: 2, z: 4, core: 2. Of those that a mesh axis runs over, the one named last changes fastest.
Arguments:
- queries: bfloat16 [4096, 5120], P(('ctx', 'tp')), may hold values from -400 to 400
- keys: bfloat16 [4096, 5120], P(('ctx', 'tp')), may hold values from -6 to 6
- values: bfloat16 [4096, 5120], P(('ctx', 'tp')), may hold values from -6 to 6
- dout: bfloat16 [4096, 5120], P(('ctx', 'tp')), may hold values from -6 to 6
- match: int32 [10, 16], replicated, may hold values from 0 to 15, as said below
Outputs:
- attended: bfloat16 [4096, 5120], P(('ctx', 'tp'))
- grad_queries: bfloat16 [4096, 5120], P(('ctx', 'tp'))
- grad_keys: bfloat16 [4096, 5120], P(('ctx', 'tp'))
- grad_values: bfloat16 [4096, 5120], P(('ctx', 'tp'))
Inputs may be any that keep to these rules, and one draw needn't show every extreme that they name: match[g, i] lies in 0 to i; the value i means that query block i has no matched block for group g. Among the 20 pairs of a query block and a group of one ctx index, at most 1 name a block of the tokens of any one other ctx index, and 1 is reached.
All inputs are finite; a program needn't handle non-finite values.
Results may differ from a plain program's by a relative error of at most 0.025.
Values may be sent and summed in bfloat16 or wider, within the bound.
A program may use at most 128 MiB of HBM per device.

v0:
```python
import functools

import jax
import jax.numpy as jnp
from jax import lax
from jax.experimental import pallas as pl
from jax.experimental.pallas import tpu as pltpu
from jax.sharding import PartitionSpec as P

HEAD_DIM = 128
BLOCK = 256
GROUPS = 10
MESH = pl.DeviceIdType.MESH
LOG2E = 1.4426950408889634


def dot(a, b, dims):
    return lax.dot_general(a, b, ((dims[:1], dims[1:]), ((), ())), preferred_element_type=jnp.float32)


def kernel(
    n,
    ctxs,
    match,
    q_ref,
    k_ref,
    v_ref,
    d_ref,
    att_ref,
    gq_ref,
    gk_ref,
    gv_ref,
    qb,
    kb,
    vb,
    db,
    attb,
    gqb,
    gkb,
    gvb,
    gk32,
    gv32,
    gfar,
    pack,
    slots,
    back,
    came,
    table,
    in_send,
    kv_recv,
    qd_recv,
    in_local,
    slot_send,
    slot_recv,
    ret_send,
    ret_recv,
    out_send,
    out_recv,
    out_local,
):
    c = lax.axis_index("ctx")
    me = lax.axis_index("tp")
    part = q_ref.shape[0]
    width = qb.shape[1]
    here = qb.shape[0] // BLOCK
    heads = width // HEAD_DIM
    shares = BLOCK // part
    peers = [lax.rem(me + d, n) for d in range(1, n)]

    def rows_of(j):
        return pl.ds(pl.multiple_of(j * part, part), part)

    def cols_of(j):
        return pl.ds(pl.multiple_of(j * width, width), width)

    def head_of(g):
        return pl.ds(pl.multiple_of(g * HEAD_DIM, HEAD_DIM), HEAD_DIM)

    def wide_head(j, g):
        return pl.ds(pl.multiple_of(j * width + g * HEAD_DIM, HEAD_DIM), HEAD_DIM)

    ins = (q_ref, k_ref, v_ref, d_ref)
    bufs = (qb, kb, vb, db)
    outs = (att_ref, gq_ref, gk_ref, gv_ref)
    stages = (attb, gqb, gkb, gvb)

    def own_in(x):
        return pltpu.make_async_copy(
            ins[x].at[:, cols_of(me)], bufs[x].at[rows_of(me), :], in_local.at[x]
        )

    for x in (0, 3):
        own_in(x).start()

    def kv_place(x, j, g):
        half = pl.multiple_of(lax.rem(j, shares) * part, part)
        return bufs[x].at[(j // shares) * heads + g, pl.ds(half, part), :]

    def own_kv(x, g):
        return pltpu.make_async_copy(
            ins[x].at[:, wide_head(me, g)], kv_place(x, me, g), in_local.at[x]
        )

    def start_own_kv(g, carry):
        for x in (1, 2):
            own_kv(x, g).start()
        return carry

    lax.fori_loop(0, heads, start_own_kv, 0)

    barrier = pltpu.get_barrier_semaphore()
    for j in peers:
        pl.semaphore_signal(barrier, inc=1, device_id=(c, j), device_id_type=MESH)

    def greet(step, carry):
        pl.semaphore_signal(
            barrier, inc=1, device_id=(lax.rem(c + step, ctxs), me), device_id_type=MESH
        )
        return carry

    lax.fori_loop(1, ctxs, greet, 0)
    pl.semaphore_wait(barrier, n - 1 + ctxs - 1)

    def kv_copy(x, j, g, row):
        return pltpu.make_async_remote_copy(
            src_ref=ins[x].at[:, wide_head(j, g)],
            dst_ref=kv_place(x, row, g),
            send_sem=in_send.at[x, j],
            recv_sem=kv_recv.at[x - 1, g, row],
            device_id=(c, j),
            device_id_type=MESH,
        )

    def send_kv(g, carry):
        for x in (1, 2):
            for j in peers:
                kv_copy(x, j, g, me).start()
        return carry

    lax.fori_loop(0, heads, send_kv, 0)

    def sent_in(x, j):
        return pltpu.make_async_remote_copy(
            src_ref=ins[x].at[:, cols_of(j)],
            dst_ref=qb.at[rows_of(me), :],
            send_sem=in_send.at[x, j],
            recv_sem=qd_recv.at[0, 0, me],
            device_id=(c, j),
            device_id_type=MESH,
        )

    def look(t, carry):
        def items(it, found):
            block, group, filled = found
            g = lax.rem(it, GROUPS)
            m = match[g, t * here + it // GROUPS]
            hit = (m >= c * here) & (m < (c + 1) * here)
            return (
                jnp.where(hit, m - c * here, block),
                jnp.where(hit, g, group),
                jnp.where(hit, 1, filled),
            )

        block, group, filled = lax.fori_loop(0, here * GROUPS, items, (0, 0, 0))
        table[0, t] = block
        table[1, t] = group
        table[2, t] = filled
        return carry

    lax.fori_loop(c + 1, ctxs, look, 0)

    def serve(s, carry):
        def items(it, found):
            m = match[lax.rem(it, GROUPS), c * here + it // GROUPS]
            hit = (m >= s * here) & (m < (s + 1) * here)
            return jnp.where(hit, it, found)

        table[3, s] = lax.fori_loop(0, here * GROUPS, items, 0)
        return carry

    lax.fori_loop(0, c, serve, 0)

    for x in (1, 2):
        for j in peers:
            sent_in(x, j).wait_send()

    def qd_copy(x, j, g, row):
        y = 0 if x == 0 else 1
        return pltpu.make_async_remote_copy(
            src_ref=ins[x].at[:, wide_head(j, g)],
            dst_ref=bufs[x].at[rows_of(row), head_of(g)],
            send_sem=in_send.at[x, j],
            recv_sem=qd_recv.at[y, g, row],
            device_id=(c, j),
            device_id_type=MESH,
        )

    def send_qd(g, carry):
        for x in (0, 3):
            for j in peers:
                qd_copy(x, j, g, me).start()
        return carry

    lax.fori_loop(0, heads, send_qd, 0)

    def take_kv(g, carry):
        for x in (1, 2):
            for j in peers:
                kv_copy(x, j, g, j).wait_recv()
        return carry

    lax.fori_loop(0, heads, take_kv, 0)
    for x in (1, 2):
        pltpu.make_async_copy(
            ins[x].at[:, cols_of(me)], qb.at[rows_of(me), :], in_local.at[x]
        ).wait()

    def slot_copy(t, s):
        return pltpu.make_async_remote_copy(
            src_ref=pack.at[t],
            dst_ref=slots.at[s],
            send_sem=slot_send.at[t],
            recv_sem=slot_recv.at[s],
            device_id=(t, me),
            device_id_type=MESH,
        )

    def send_slot(t, carry):
        item = table[0, t] * heads + table[1, t]
        pack[t, 0] = kb[item]
        pack[t, 1] = vb[item]
        slot_copy(t, c).start()
        return carry

    lax.fori_loop(c + 1, ctxs, send_slot, 0)

    own_in(0).wait()
    own_in(3).wait()

    def take_slot(s, carry):
        slot_copy(s, s).wait_recv()
        return carry

    lax.fori_loop(0, c, take_slot, 0)

    scale = HEAD_DIM**-0.5
    key_at = lax.broadcasted_iota(jnp.int32, (BLOCK, BLOCK), 0)
    query_at = lax.broadcasted_iota(jnp.int32, (BLOCK, BLOCK), 1)

    def out_copy(o, j, g, col):
        return pltpu.make_async_remote_copy(
            src_ref=stages[o].at[rows_of(j), head_of(g)],
            dst_ref=outs[o].at[:, wide_head(col, g)],
            send_sem=out_send.at[o, j],
            recv_sem=out_recv.at[o, col],
            device_id=(c, j),
            device_id_type=MESH,
        )

    def own_out(o, g):
        return pltpu.make_async_copy(
            stages[o].at[rows_of(me), head_of(g)], outs[o].at[:, wide_head(me, g)], out_local.at[o]
        )

    def send_out(o, g):
        for j in peers:
            out_copy(o, j, g, me).start()
        own_out(o, g).start()

    def work(g, carry):
        for x in (0, 3):
            for j in peers:
                qd_copy(x, j, g, j).wait_recv()
        cols = head_of(g)
        totals = []
        for b in range(here):
            rows = pl.ds(b * BLOCK, BLOCK)
            q, do = qb[rows, cols], db[rows, cols]
            k, v = kb[b * heads + g], vb[b * heads + g]
            m = match[g, c * here + b]
            valid = m < c * here + b
            source = lax.div(m, here)
            fk, fv = slots[source, 0], slots[source, 1]
            for near in range(b + 1):
                hit = m == c * here + near
                fk = jnp.where(hit, kb[near * heads + g], fk)
                fv = jnp.where(hit, vb[near * heads + g], fv)
            s_own = jnp.where(key_at <= query_at, dot(k, q, (1, 1)) * (scale * LOG2E), -jnp.inf)
            s_far = dot(fk, q, (1, 1)) * (scale * LOG2E) + jnp.where(valid, 0.0, -jnp.inf)
            top = jnp.maximum(
                jnp.max(s_own, axis=0, keepdims=True), jnp.max(s_far, axis=0, keepdims=True)
            )
            e_own = jnp.exp2(s_own - top)
            e_far = jnp.exp2(s_far - top)
            inverse = 1.0 / (
                jnp.sum(e_own, axis=0, keepdims=True) + jnp.sum(e_far, axis=0, keepdims=True)
            )
            p_own = e_own * inverse
            p_far = e_far * inverse
            pb_own = p_own.astype(jnp.bfloat16)
            pb_far = p_far.astype(jnp.bfloat16)
            att = (dot(v, pb_own, (0, 0)) + dot(fv, pb_far, (0, 0))).astype(jnp.bfloat16)
            att = att.astype(jnp.float32)
            delta = jnp.sum(do.astype(jnp.float32).T * att, axis=0, keepdims=True)
            attb[rows, cols] = att.T.astype(jnp.bfloat16)
            ds_own = (p_own * (dot(v, do, (1, 1)) - delta) * scale).astype(jnp.bfloat16)
            ds_far = (p_far * (dot(fv, do, (1, 1)) - delta) * scale).astype(jnp.bfloat16)
            gq = dot(k, ds_own, (0, 0)) + dot(fk, ds_far, (0, 0))
            gqb[rows, cols] = gq.T.astype(jnp.bfloat16)
            gk_far = dot(ds_far, q, (1, 0))
            gv_far = dot(pb_far, do, (1, 0))
            gfar[b * GROUPS + g, 0] = gk_far.astype(jnp.bfloat16)
            gfar[b * GROUPS + g, 1] = gv_far.astype(jnp.bfloat16)
            gk32[rows, cols] = dot(ds_own, q, (1, 0))
            gv32[rows, cols] = dot(pb_own, do, (1, 0))
            for target in range(b):
                hit = m == c * here + target
                to = pl.ds(target * BLOCK, BLOCK)
                gk32[to, cols] += jnp.where(hit, gk_far, 0.0)
                gv32[to, cols] += jnp.where(hit, gv_far, 0.0)
        send_out(0, g)
        send_out(1, g)
        return carry

    lax.fori_loop(0, heads, work, 0)

    def ret_copy(s, t):
        return pltpu.make_async_remote_copy(
            src_ref=back.at[s],
            dst_ref=came.at[t],
            send_sem=ret_send.at[s],
            recv_sem=ret_recv.at[t],
            device_id=(s, me),
            device_id_type=MESH,
        )

    def send_back(s, carry):
        item = table[3, s]
        back[s, 0] = gfar[item, 0]
        back[s, 1] = gfar[item, 1]
        ret_copy(s, c).start()
        return carry

    lax.fori_loop(0, c, send_back, 0)

    def take_back(t, carry):
        ret_copy(t, t).wait_recv()
        return carry

    lax.fori_loop(c + 1, ctxs, take_back, 0)

    def finish(g, carry):
        cols = head_of(g)
        for b in range(here):
            rows = pl.ds(b * BLOCK, BLOCK)
            for x, total, stage in ((0, gk32, gkb), (1, gv32, gvb)):

                def add(t, held):
                    hit = (table[0, t] == b) & (table[1, t] == g) & (table[2, t] == 1)
                    return held + jnp.where(hit, came[t, x].astype(jnp.float32), 0.0)

                stage[rows, cols] = lax.fori_loop(c + 1, ctxs, add, total[rows, cols]).astype(
                    jnp.bfloat16
                )
        send_out(2, g)
        send_out(3, g)
        return carry

    lax.fori_loop(0, heads, finish, 0)

    for x in (0, 3):
        for j in peers:
            sent_in(x, j).wait_send()

    def slots_sent(t, carry):
        slot_copy(t, c).wait_send()
        return carry

    lax.fori_loop(c + 1, ctxs, slots_sent, 0)

    def backs_sent(s, carry):
        ret_copy(s, c).wait_send()
        return carry

    lax.fori_loop(0, c, backs_sent, 0)
    for o in range(4):
        pltpu.make_async_copy(
            stages[o].at[rows_of(me), :], outs[o].at[:, cols_of(me)], out_local.at[o]
        ).wait()
        for j in peers:
            whole = pltpu.make_async_remote_copy(
                src_ref=stages[o].at[rows_of(j), :],
                dst_ref=outs[o].at[:, cols_of(j)],
                send_sem=out_send.at[o, j],
                recv_sem=out_recv.at[o, j],
                device_id=(c, j),
                device_id_type=MESH,
            )
            whole.wait_send()
            whole.wait_recv()


def solution(mesh):
    n = mesh.shape["tp"]
    ctxs = mesh.shape["ctx"]

    def shards(queries, keys, values, dout, match):
        part, width_all = queries.shape
        tokens, width = part * n, width_all // n
        here = tokens // BLOCK
        heads = width // HEAD_DIM
        assert heads == GROUPS
        buf = pltpu.VMEM((tokens, width), jnp.bfloat16)
        tiles = pltpu.VMEM((here * heads, BLOCK, HEAD_DIM), jnp.bfloat16)
        wide = pltpu.VMEM((tokens, width), jnp.float32)
        pairs = pltpu.VMEM((ctxs, 2, BLOCK, HEAD_DIM), jnp.bfloat16)
        dma = pltpu.SemaphoreType.DMA
        anywhere = pl.BlockSpec(memory_space=pl.ANY)
        items = here * heads
        return pl.pallas_call(
            functools.partial(kernel, n, ctxs),
            out_shape=[jax.ShapeDtypeStruct((part, width_all), jnp.bfloat16)] * 4,
            in_specs=[pl.BlockSpec(memory_space=pltpu.SMEM)] + [anywhere] * 4,
            out_specs=[anywhere] * 4,
            scratch_shapes=[buf, tiles, tiles, buf]
            + [buf] * 4
            + [wide] * 2
            + [pltpu.VMEM((items, 2, BLOCK, HEAD_DIM), jnp.bfloat16)]
            + [pairs] * 4
            + [
                pltpu.SMEM((4, ctxs), jnp.int32),
                dma((4, n)),
                dma((2, heads, n)),
                dma((2, heads, n)),
                dma((4,)),
                dma((ctxs,)),
                dma((ctxs,)),
                dma((ctxs,)),
                dma((ctxs,)),
                dma((4, n)),
                dma((4, n)),
                dma((4,)),
            ],
            compiler_params=pltpu.CompilerParams(
                collective_id=0, has_side_effects=True, vmem_limit_bytes=56 * 1024 * 1024
            ),
            cost_estimate=pl.CostEstimate(
                flops=12 * items * 2 * BLOCK * BLOCK * HEAD_DIM,
                bytes_accessed=16 * tokens * width,
                transcendentals=2 * items * BLOCK * BLOCK,
            ),
            name="matched_blocks",
        )(match, queries, keys, values, dout)

    split = P(("ctx", "tp"), None)
    return jax.shard_map(
        shards,
        mesh=mesh,
        in_specs=(split, split, split, split, P()),
        out_specs=(split,) * 4,
        check_vma=False,
    )
```

profile of v0, /device:TPU:23, one launch (start us, length us, event | category | flops | bytes accessed | tf_op | source)
XLA Modules:
  0.0 136.2 jit_solution(4248755623343814646)
XLA Ops:
  0.6 128.3 %matched_blocks.1 = (bf16[128,5120]{1,0:T(8,128)(2,1)}, bf16[128,5120]{1,0:T(8,128)(2,1)}, bf16[128,5120]{1,0:T(8,128)(2,1)}, bf16[128,5120]{1,0:T(8,128)(2,1)}) custom-call(s32[10,16]{1,0:T(8,128)} %match.1, bf16[128,5120]{1,0:T(8,128)(2,1)} %q_ref.1, bf16[128,5120]{1,0:T(8,128)(2,1)} %k_ref.1, bf16[128,5120]{1,0:T(8,128)(2,1)} %v_ref.1, ...), custom_call_target="tpu_custom_call" | custom-call | flops 4026531840 | bytes 10485760 | tf_op jit(solution)/shard_map/matched_blocks/pallas_call | solution.py:420
  129.0 0.0 copy-start.2
  129.0 2.6 %copy.13 = bf16[128,5120]{1,0:T(8,128)(2,1)} copy(bf16[128,5120]{1,0:T(8,128)(2,1)} %get-tuple-element.8) | data formatting | bytes 2621440
  131.5 0.0 copy-done.2
  131.5 0.0 copy-start.1
  131.5 1.1 copy.14
  132.6 0.7 copy-done.1
  133.3 0.0 copy-start
  133.3 1.1 copy.15
  134.4 0.7 copy-done
  135.1 1.1 copy.16
Async XLA Ops:
  129.0 2.6 %copy-start.2 = (bf16[128,5120]{1,0:T(8,128)(2,1)S(1)}, bf16[128,5120]{1,0:T(8,128)(2,1)}, u32[]{:S(2)}) copy-start(bf16[128,5120]{1,0:T(8,128)(2,1)} %get-tuple-element.9) | copy-start | bytes 3932164
  131.5 1.8 %copy-start.1 = (bf16[128,5120]{1,0:T(8,128)(2,1)S(1)}, bf16[128,5120]{1,0:T(8,128)(2,1)}, u32[]{:S(2)}) copy-start(bf16[128,5120]{1,0:T(8,128)(2,1)} %get-tuple-element.10) | copy-start | bytes 3932164
  133.3 1.8 %copy-start = (bf16[128,5120]{1,0:T(8,128)(2,1)S(1)}, bf16[128,5120]{1,0:T(8,128)(2,1)}, u32[]{:S(2)}) copy-start(bf16[128,5120]{1,0:T(8,128)(2,1)} %get-tuple-element.11) | copy-start | bytes 3932164
where the time goes:
time: 136 us
  Pallas kernels  128 us (94%)
  local copies, waits for them, and re-layouts  7.2 us (5%)
    pallas_call x1, Pallas kernels, shards(): pl.pallas_call(functools.partial(kernel, n, ctxs), out_shape=[jax.ShapeDt...  128 us
    unnamed x10, local copies, waits for them, and re-layouts  7.2 us

commit v1 on v0

--- a/solution.py
+++ b/solution.py
@@ -84,6 +84,17 @@
     outs = (att_ref, gq_ref, gk_ref, gv_ref)
     stages = (attb, gqb, gkb, gvb)
 
+    barrier = pltpu.get_barrier_semaphore()
+    for j in peers:
+        pl.semaphore_signal(barrier, inc=1, device_id=(c, j), device_id_type=MESH)
+
+    def greet(step, carry):
+        pl.semaphore_signal(
+            barrier, inc=1, device_id=(lax.rem(c + step, ctxs), me), device_id_type=MESH
+        )
+        return carry
+
+    lax.fori_loop(1, ctxs, greet, 0)
     def own_in(x):
         return pltpu.make_async_copy(
             ins[x].at[:, cols_of(me)], bufs[x].at[rows_of(me), :], in_local.at[x]
@@ -108,17 +119,6 @@
 
     lax.fori_loop(0, heads, start_own_kv, 0)
 
-    barrier = pltpu.get_barrier_semaphore()
-    for j in peers:
-        pl.semaphore_signal(barrier, inc=1, device_id=(c, j), device_id_type=MESH)
-
-    def greet(step, carry):
-        pl.semaphore_signal(
-            barrier, inc=1, device_id=(lax.rem(c + step, ctxs), me), device_id_type=MESH
-        )
-        return carry
-
-    lax.fori_loop(1, ctxs, greet, 0)
     pl.semaphore_wait(barrier, n - 1 + ctxs - 1)
 
     def kv_copy(x, j, g, row):
@@ -148,6 +148,27 @@
             device_id=(c, j),
             device_id_type=MESH,
         )
+
+    def qd_copy(x, j, g, row):
+        y = 0 if x == 0 else 1
+        return pltpu.make_async_remote_copy(
+            src_ref=ins[x].at[:, wide_head(j, g)],
+            dst_ref=bufs[x].at[rows_of(row), head_of(g)],
+            send_sem=in_send.at[x, j],
+            recv_sem=qd_recv.at[y, g, row],
+            device_id=(c, j),
+            device_id_type=MESH,
+        )
+
+    def send_qd(g, carry):
+        for x in (0, 3):
+            for j in peers:
+                qd_copy(x, j, g, me).start()
+        return carry
+
+    for j in peers:
+        sent_in(1, j).wait_send()
+    lax.fori_loop(0, heads, send_qd, 0)
 
     def look(t, carry):
         def items(it, found):
@@ -179,29 +200,6 @@
         return carry
 
     lax.fori_loop(0, c, serve, 0)
-
-    for x in (1, 2):
-        for j in peers:
-            sent_in(x, j).wait_send()
-
-    def qd_copy(x, j, g, row):
-        y = 0 if x == 0 else 1
-        return pltpu.make_async_remote_copy(
-            src_ref=ins[x].at[:, wide_head(j, g)],
-            dst_ref=bufs[x].at[rows_of(row), head_of(g)],
-            send_sem=in_send.at[x, j],
-            recv_sem=qd_recv.at[y, g, row],
-            device_id=(c, j),
-            device_id_type=MESH,
-        )
-
-    def send_qd(g, carry):
-        for x in (0, 3):
-            for j in peers:
-                qd_copy(x, j, g, me).start()
-        return carry
-
-    lax.fori_loop(0, heads, send_qd, 0)
 
     def take_kv(g, carry):
         for x in (1, 2):
@@ -368,7 +366,7 @@
 
     lax.fori_loop(0, heads, finish, 0)
 
-    for x in (0, 3):
+    for x in (0, 2, 3):
         for j in peers:
             sent_in(x, j).wait_send()
 
@@ -417,6 +415,7 @@
         dma = pltpu.SemaphoreType.DMA
         anywhere = pl.BlockSpec(memory_space=pl.ANY)
         items = here * heads
+        held = tokens * width * 24 + (items + 4 * ctxs) * 2 * BLOCK * HEAD_DIM * 2
         return pl.pallas_call(
             functools.partial(kernel, n, ctxs),
             out_shape=[jax.ShapeDtypeStruct((part, width_all), jnp.bfloat16)] * 4,
@@ -442,7 +441,7 @@
                 dma((4,)),
             ],
             compiler_params=pltpu.CompilerParams(
-                collective_id=0, has_side_effects=True, vmem_limit_bytes=56 * 1024 * 1024
+                collective_id=0, has_side_effects=True, vmem_limit_bytes=held + 9 * 1024 * 1024
             ),
             cost_estimate=pl.CostEstimate(
                 flops=12 * items * 2 * BLOCK * BLOCK * HEAD_DIM,
@@ -450,7 +449,10 @@
                 transcendentals=2 * items * BLOCK * BLOCK,
             ),
             name="matched_blocks",
-        )(match, queries, keys, values, dout)
+        )(
+            match,
+            *(pltpu.with_memory_space_constraint(x, pltpu.HBM) for x in (queries, keys, values, dout)),
+        )
 
     split = P(("ctx", "tp"), None)
     return jax.shard_map(

time: 136 us -> 132 us (0.971)
  local copies, waits for them, and re-layouts: 7.2 us -> 4.92 us
  Pallas kernels: 128 us -> 126 us
    unnamed x10 -> x6, local copies, waits for them, and re-layouts: 7.2 us -> 4.92 us
    pallas_call x1, Pallas kernels: 128 us -> 126 us  [shards(): pl.pallas_call(functools.partial(kernel, n, ctxs), out_shape=[jax.ShapeDt...]
where the time goes in v1:
time: 132 us
  Pallas kernels  126 us (95%)
  local copies, waits for them, and re-layouts  4.92 us (4%)
    pallas_call x1, Pallas kernels, shards(): pl.pallas_call(functools.partial(kernel, n, ctxs), out_shape=[jax.ShapeDt...  126 us
    unnamed x6, local copies, waits for them, and re-layouts  4.92 us

profile of v1, /device:TPU:23, one launch (start us, length us, event | category | flops | bytes accessed | tf_op | source)
XLA Modules:
  0.0 131.7 jit_solution(8991128778324910833)
XLA Ops:
  0.6 0.0 copy-start
  0.6 0.7 copy-done
  1.3 126.1 %matched_blocks.1 = (bf16[128,5120]{1,0:T(8,128)(2,1)S(1)}, bf16[128,5120]{1,0:T(8,128)(2,1)S(1)}, bf16[128,5120]{1,0:T(8,128)(2,1)S(1)}, bf16[128,5120]{1,0:T(8,128)(2,1)S(1)}) custom-call(s32[10,16]{1,0:T(8,128)S(1)} %copy-done, bf16[128,5120]{1,0:T(8,128)(2,1)} %q_ref.1, bf16[128,5120]{1,0:T(8,128)(2,1)} %k_ref.1, bf16[128,5120]{1,0:T(8,128)(2,1)} %v_ref.1, ...), custom_call_target="tpu_custom_call" | custom-call | flops 4026531840 | bytes 10485760 | tf_op jit(solution)/shard_map/matched_blocks/pallas_call | solution.py:419
  127.5 1.1 copy.13
  128.5 1.1 copy.14
  129.6 1.1 copy.15
  130.6 1.1 copy.16
Async XLA Ops:
  0.6 0.7 copy-start
